TPU v7x, 512 devices: a whole 4x8x8 slice. The times are simulated.
512 devices in a mesh: blk: 32 (over x, y_lo, core), uly: 16 (over y_hi, z).
Axes of the slice: x: 4, y: 8 (y_hi: 2, y_lo: 4; y = y_hi * 4 + y_lo), z: 8, core: 2. Of those that a mesh axis runs over, the one named last changes fastest.
Arguments:
- query_in: bfloat16 [65536, 4096], P(('blk', 'uly')), may hold values from -16 to 16, as said below
- key_in: bfloat16 [65536, 2048], P(('blk', 'uly')), may hold values from -16 to 16, as said below
- value_in: bfloat16 [65536, 2048], P(('blk', 'uly')), may hold values from -6 to 6
- grad_out: bfloat16 [65536, 4096], P(('blk', 'uly')), may hold values from -6 to 6
- row_dot: bfloat16 [65536, 16], P(('blk', 'uly')), may hold values from -96 to 96
- segments: int32 [65536], replicated, may hold values from 0 to 15, never falling along the last dimension, each value on 1 to 8192 neighbouring positions
Outputs:
- grad_query: bfloat16 [65536, 4096], P(('blk', 'uly'))
- grad_key: bfloat16 [65536, 2048], P(('blk', 'uly'))
- grad_value: bfloat16 [65536, 2048], P(('blk', 'uly'))
Inputs may be any that keep to these rules, and one draw needn't show every extreme that they name: `query_in`: queries: entries of independent magnitude, each token and head with its own scale. `key_in`: keys: entries of independent magnitude, each token and head with its own scale.
All inputs are finite; a program needn't handle non-finite values.
Results may differ from a plain program's by a relative error of at most 0.006.
Values may be sent and summed in bfloat16 or wider, within the bound.
A program may use at most 64 MiB of HBM per device.

v0:
```python
import jax
import jax.numpy as jnp
from jax import lax
from jax.sharding import PartitionSpec as P

HEADS = 16
KV_HEADS = 8
HEAD_DIM = 256
WINDOW = 512


query_scale = 0.0625
soft_cap = 50.0


def from_behind(array, axis, by):
    size = lax.axis_size(axis)
    pairs = [(i, i + by) for i in range(size) if 0 <= i + by < size]
    return lax.ppermute(array, axis, pairs)


def allow_pairs(query_pos, key_pos, query_seg, key_seg):
    spacing = query_pos[:, None] - key_pos[None, :]
    return (
        (spacing >= 0)
        & (spacing < WINDOW)
        & (key_pos[None, :] >= 0)
        & (query_seg[:, None] == key_seg[None, :])
    )


def forward_tile(query_tile, keys, allowed):
    raw_score = (
        jnp.einsum("qhd,khd->hqk", query_tile, keys, preferred_element_type=jnp.float32)
        * query_scale
    )
    bent_score = jnp.tanh(raw_score / soft_cap)
    weight = jnp.where(allowed[None], jnp.exp(soft_cap * bent_score), jnp.zeros_like(bent_score))
    return (bent_score, weight)


def backward_tile(weight, bent_score, row_total, query_tile, grad_tile, offsets, keys, values):
    prob_full = weight / row_total[:, :, None]
    prob_low = prob_full.astype(jnp.bfloat16)
    value_grad = jnp.einsum("hqk,qhd->khd", prob_low, grad_tile, preferred_element_type=jnp.float32)
    grad_prob = jnp.einsum("qhd,khd->hqk", grad_tile, values, preferred_element_type=jnp.float32)
    grad_score = (
        prob_full * (grad_prob - offsets[:, :, None]) * (1.0 - bent_score * bent_score)
    ).astype(jnp.bfloat16)
    query_grad = (
        jnp.einsum("hqk,khd->qhd", grad_score, keys, preferred_element_type=jnp.float32)
        * query_scale
    )
    key_grad = (
        jnp.einsum("hqk,qhd->khd", grad_score, query_tile, preferred_element_type=jnp.float32)
        * query_scale
    )
    return (query_grad, key_grad, value_grad)


def per_device(query_in, key_in, value_in, grad_out, row_dot, segments):
    rows_here = query_in.shape[0]
    groups = HEADS // KV_HEADS
    block_len = rows_here * lax.axis_size("uly")
    tile = min(512, block_len)
    reach = WINDOW
    block_first = lax.axis_index("blk") * block_len
    query_heads = query_in.reshape(rows_here, HEADS, HEAD_DIM)
    key_heads = jnp.repeat(key_in.reshape(rows_here, KV_HEADS, HEAD_DIM), groups, axis=1)
    value_heads = jnp.repeat(value_in.reshape(rows_here, KV_HEADS, HEAD_DIM), groups, axis=1)
    grad_heads = grad_out.reshape(rows_here, HEADS, HEAD_DIM)
    query_local, key_local, value_local, grad_local, row_sums = (
        lax.all_to_all(query_heads, "uly", split_axis=1, concat_axis=0, tiled=True),
        lax.all_to_all(key_heads, "uly", split_axis=1, concat_axis=0, tiled=True),
        lax.all_to_all(value_heads, "uly", split_axis=1, concat_axis=0, tiled=True),
        lax.all_to_all(grad_heads, "uly", split_axis=1, concat_axis=0, tiled=True),
        lax.all_to_all(row_dot, "uly", split_axis=1, concat_axis=0, tiled=True),
    )
    offsets = row_sums.astype(jnp.float32).T
    seg_pad = jnp.concatenate(
        [jnp.full((reach,), -1, jnp.int32), segments, jnp.full((reach,), -1, jnp.int32)], axis=0
    )
    own_seg = lax.dynamic_slice_in_dim(seg_pad, block_first + reach, block_len)
    parts = []
    tail = jnp.stack([key_local[block_len - reach :], value_local[block_len - reach :]])
    prior = from_behind(tail, "blk", 1)
    key_ext = jnp.concatenate([prior[0], key_local], axis=0)
    value_ext = jnp.concatenate([prior[1], value_local], axis=0)
    ext_seg = lax.dynamic_slice_in_dim(seg_pad, block_first, reach + block_len)
    key_acc = jnp.zeros((reach + block_len,) + key_local.shape[1:], jnp.float32)
    value_acc = jnp.zeros((reach + block_len,) + key_local.shape[1:], jnp.float32)
    for start in range(0, block_len, tile):
        stop = start + tile
        query_pos = block_first + start + jnp.arange(tile, dtype=jnp.int32)
        key_pos = block_first - reach + start + jnp.arange(tile + reach, dtype=jnp.int32)
        allowed = allow_pairs(
            query_pos, key_pos, own_seg[start:stop], ext_seg[start : stop + reach]
        )
        keys = key_ext[start : stop + reach]
        values = value_ext[start : stop + reach]
        bent_score, weight = forward_tile(query_local[start:stop], keys, allowed)
        row_total = jnp.sum(weight, axis=2)
        query_grad, key_grad, value_grad = backward_tile(
            weight,
            bent_score,
            row_total,
            query_local[start:stop],
            grad_local[start:stop],
            offsets[:, start:stop],
            keys,
            values,
        )
        parts.append(query_grad)
        key_acc = key_acc.at[start : stop + reach].add(key_grad)
        value_acc = value_acc.at[start : stop + reach].add(value_grad)
    returned = from_behind(jnp.stack([key_acc[:reach], value_acc[:reach]]), "blk", -1)
    own_key = key_acc[reach:].at[block_len - reach :].add(returned[0])
    own_value = value_acc[reach:].at[block_len - reach :].add(returned[1])
    query_all = jnp.concatenate(parts, axis=0).astype(jnp.bfloat16)
    query_back, key_back, value_back = (
        lax.all_to_all(query_all, "uly", split_axis=0, concat_axis=1, tiled=True),
        lax.all_to_all(
            own_key.astype(jnp.bfloat16), "uly", split_axis=0, concat_axis=1, tiled=True
        ),
        lax.all_to_all(
            own_value.astype(jnp.bfloat16), "uly", split_axis=0, concat_axis=1, tiled=True
        ),
    )
    grad_query = query_back.reshape(rows_here, HEADS * HEAD_DIM)
    key_sum = (
        lax.optimization_barrier(key_back)
        .astype(jnp.float32)
        .reshape(rows_here, KV_HEADS, groups, HEAD_DIM)
        .sum(axis=2)
    )
    value_sum = (
        lax.optimization_barrier(value_back)
        .astype(jnp.float32)
        .reshape(rows_here, KV_HEADS, groups, HEAD_DIM)
        .sum(axis=2)
    )
    grad_key = key_sum.astype(jnp.bfloat16).reshape(rows_here, KV_HEADS * HEAD_DIM)
    grad_value = value_sum.astype(jnp.bfloat16).reshape(rows_here, KV_HEADS * HEAD_DIM)
    return (grad_query, grad_key, grad_value)


def solution(mesh):
    in_specs = (
        P(("blk", "uly"), None),
        P(("blk", "uly"), None),
        P(("blk", "uly"), None),
        P(("blk", "uly"), None),
        P(("blk", "uly"), None),
        P(),
    )
    out_specs = (P(("blk", "uly"), None), P(("blk", "uly"), None), P(("blk", "uly"), None))
    return jax.shard_map(
        per_device, mesh=mesh, in_specs=in_specs, out_specs=out_specs, check_vma=False
    )
```

profile of v0, /device:TPU:40, one launch (start us, length us, event | category | flops | bytes accessed | tf_op | source)
XLA Modules:
  0.0 343.1 jit_solution(17430735291768610181)
XLA Ops:
  1.9 15.7 %all-to-all-start.4 = ((bf16[128,16,1]{0,2,1:T(2,128)(2,1)}), bf16[128,16,1]{0,2,1:T(2,128)(2,1)S(1)}, u32[]{:S(2)}, u32[]{:S(2)}) async-start(bf16[128,16,1]{0,2,1:T(2,128)(2,1)} %copy.115), calls=%async_computation.4 | async-start | bytes 16384 | tf_op jit(solution)/shard_map/all_to_all | solution.py:77
  18.7 5.9 %all-to-all-done.4 = bf16[128,16,1]{0,2,1:T(2,128)(2,1)S(1)} async-done(((bf16[128,16,1]{0,2,1:T(2,128)(2,1)}), bf16[128,16,1]{0,2,1:T(2,128)(2,1)S(1)}, u32[]{:S(2)}, u32[]{:S(2)}) %all-to-all-start.4) | async-done | bytes 4128 | tf_op jit(solution)/shard_map/all_to_all | solution.py:77
  25.7 8.9 %all-to-all-start = ((bf16[128,16,256]{2,0,1:T(8,128)(2,1)}), bf16[128,16,256]{2,0,1:T(8,128)(2,1)S(1)}, u32[]{:S(2)}, u32[]{:S(2)}) async-start(bf16[128,16,256]{2,0,1:T(8,128)(2,1)} %bitcast), calls=%async_computation | async-start | bytes 2097152 | tf_op jit(solution)/shard_map/all_to_all | solution.py:74
  34.6 27.5 %all-to-all-done = bf16[128,16,256]{2,0,1:T(8,128)(2,1)S(1)} async-done(((bf16[128,16,256]{2,0,1:T(8,128)(2,1)}), bf16[128,16,256]{2,0,1:T(8,128)(2,1)S(1)}, u32[]{:S(2)}, u32[]{:S(2)}) %all-to-all-start) | async-done | bytes 1048608 | tf_op jit(solution)/shard_map/all_to_all | solution.py:74
  63.2 11.4 %all-to-all-start.1 = ((bf16[128,16,256]{2,0,1:T(8,128)(2,1)}), bf16[128,16,256]{2,0,1:T(8,128)(2,1)S(1)}, u32[]{:S(2)}, u32[]{:S(2)}) async-start(bf16[128,16,256]{2,0,1:T(8,128)(2,1)} %bitcast.4), calls=%async_computation.1 | async-start | bytes 2097152 | tf_op jit(solution)/shard_map/all_to_all | solution.py:75
  75.9 26.5 %all-to-all-done.1 = bf16[128,16,256]{2,0,1:T(8,128)(2,1)S(1)} async-done(((bf16[128,16,256]{2,0,1:T(8,128)(2,1)}), bf16[128,16,256]{2,0,1:T(8,128)(2,1)S(1)}, u32[]{:S(2)}, u32[]{:S(2)}) %all-to-all-start.1) | async-done | bytes 1048608 | tf_op jit(solution)/shard_map/all_to_all | solution.py:75
  102.4 11.8 %all-to-all-start.2 = ((bf16[128,16,256]{0,2,1:T(8,128)(2,1)}), bf16[128,16,256]{0,2,1:T(8,128)(2,1)S(1)}, u32[]{:S(2)}, u32[]{:S(2)}) async-start(bf16[128,16,256]{0,2,1:T(8,128)(2,1)} %bitcast.254), calls=%async_computation.2 | async-start | bytes 2097152 | tf_op jit(solution)/shard_map/all_to_all | solution.py:73
  114.3 2.3 copy.113
  117.6 22.6 %all-to-all-done.2 = bf16[128,16,256]{0,2,1:T(8,128)(2,1)S(1)} async-done(((bf16[128,16,256]{0,2,1:T(8,128)(2,1)}), bf16[128,16,256]{0,2,1:T(8,128)(2,1)S(1)}, u32[]{:S(2)}, u32[]{:S(2)}) %all-to-all-start.2) | async-done | bytes 1048608 | tf_op jit(solution)/shard_map/all_to_all | solution.py:73
  140.3 10.8 %all-to-all-start.3 = ((bf16[128,16,256]{0,2,1:T(8,128)(2,1)}), bf16[128,16,256]{0,2,1:T(8,128)(2,1)}, u32[]{:S(2)}, u32[]{:S(2)}) async-start(bf16[128,16,256]{0,2,1:T(8,128)(2,1)} %bitcast.253), calls=%async_computation.3 | async-start | bytes 2097152 | tf_op jit(solution)/shard_map/all_to_all | solution.py:76
  163.4 17.1 %all-to-all-done.3 = bf16[128,16,256]{0,2,1:T(8,128)(2,1)} async-done(((bf16[128,16,256]{0,2,1:T(8,128)(2,1)}), bf16[128,16,256]{0,2,1:T(8,128)(2,1)}, u32[]{:S(2)}, u32[]{:S(2)}) %all-to-all-start.3) | async-done | bytes 1048608 | tf_op jit(solution)/shard_map/all_to_all | solution.py:76
  186.8 2.8 fusion.52
  189.7 2.2 multiply_convert_fusion.1
  193.4 2.2 multiply_convert_fusion.2
  197.1 2.2 multiply_convert_fusion
  203.3 2.8 convolution_bitcast_fusion.3
  206.0 3.2 fusion
  213.9 11.2 %all-to-all-start.5 = ((bf16[16,2,16384]{2,1,0:T(2,128)(2,1)}), bf16[16,2,16384]{2,1,0:T(2,128)(2,1)S(1)}, u32[]{:S(2)}, u32[]{:S(2)}) async-start(bf16[16,2,16384]{2,1,0:T(2,128)(2,1)} %reshape.765), calls=%async_computation.5 | async-start | bytes 2097152 | tf_op jit(solution)/shard_map/all_to_all | solution.py:121
  239.1 12.1 %collective-permute-done.1 = f32[2,512,1,256]{3,1,2,0:T(8,128)S(1)} collective-permute-done((f32[2,512,1,256]{3,1,2,0:T(8,128)S(1)}, f32[2,512,1,256]{3,1,2,0:T(8,128)S(1)}, u32[]{:S(2)}, u32[]{:S(2)}) %collective-permute-start.1) | collective-permute-done | bytes 1048608 | tf_op jit(solution)/shard_map/ppermute | solution.py:19
  255.5 12.0 %all-to-all-start.6 = ((bf16[16,2,16384]{2,1,0:T(2,128)(2,1)}), bf16[16,2,16384]{2,1,0:T(2,128)(2,1)S(1)}, u32[]{:S(2)}, u32[]{:S(2)}) async-start(bf16[16,2,16384]{2,1,0:T(2,128)(2,1)} %reshape.767), calls=%async_computation.6 | async-start | bytes 2097152 | tf_op jit(solution)/shard_map/all_to_all | solution.py:122
  271.8 23.5 %all-to-all-done.6 = bf16[16,2,16384]{2,1,0:T(2,128)(2,1)S(1)} async-done(((bf16[16,2,16384]{2,1,0:T(2,128)(2,1)}), bf16[16,2,16384]{2,1,0:T(2,128)(2,1)S(1)}, u32[]{:S(2)}, u32[]{:S(2)}) %all-to-all-start.6) | async-done | bytes 1048608 | tf_op jit(solution)/shard_map/all_to_all | solution.py:122
  296.2 12.5 %all-to-all-start.7 = ((bf16[16,2,16384]{2,1,0:T(2,128)(2,1)}), bf16[16,2,16384]{2,1,0:T(2,128)(2,1)}, u32[]{:S(2)}, u32[]{:S(2)}) async-start(bf16[16,2,16384]{2,1,0:T(2,128)(2,1)} %reshape.769), calls=%async_computation.7 | async-start | bytes 2097152 | tf_op jit(solution)/shard_map/all_to_all | solution.py:125
  316.6 20.5 %all-to-all-done.7 = bf16[16,2,16384]{2,1,0:T(2,128)(2,1)} async-done(((bf16[16,2,16384]{2,1,0:T(2,128)(2,1)}), bf16[16,2,16384]{2,1,0:T(2,128)(2,1)}, u32[]{:S(2)}, u32[]{:S(2)}) %all-to-all-start.7) | async-done | bytes 1048608 | tf_op jit(solution)/shard_map/all_to_all | solution.py:125
  337.1 4.3 %reshape.770 = bf16[2048,1,256]{2,1,0:T(2,128)(2,1)S(1)} reshape(bf16[16,2,16384]{2,1,0:T(2,128)(2,1)} %all-to-all-done.7) | data formatting | bytes 2097152
  (160 shorter events, 69.7 us)
Async XLA Ops:
  1.9 22.7 %all-to-all-start.4 = ((bf16[128,16,1]{0,2,1:T(2,128)(2,1)}), bf16[128,16,1]{0,2,1:T(2,128)(2,1)S(1)}, u32[]{:S(2)}, u32[]{:S(2)}) async-start(bf16[128,16,1]{0,2,1:T(2,128)(2,1)} %copy.115), calls=%async_computation.4 | async-start | bytes 16384 | tf_op jit(solution)/shard_map/all_to_all | solution.py:77
  18.7 15.9 %copy-start.16 = (bf16[128,2048]{1,0:T(8,128)(2,1)S(1)}, bf16[128,2048]{1,0:T(8,128)(2,1)}, u32[]{:S(2)}) copy-start(bf16[128,2048]{1,0:T(8,128)(2,1)} %param.28) | copy-start | bytes 1572868
  25.7 36.4 %all-to-all-start = ((bf16[128,16,256]{2,0,1:T(8,128)(2,1)}), bf16[128,16,256]{2,0,1:T(8,128)(2,1)S(1)}, u32[]{:S(2)}, u32[]{:S(2)}) async-start(bf16[128,16,256]{2,0,1:T(8,128)(2,1)} %bitcast), calls=%async_computation | async-start | bytes 2097152 | tf_op jit(solution)/shard_map/all_to_all | solution.py:74
  34.6 40.0 %copy-start.2 = (bf16[128,4096]{1,0:T(8,128)(2,1)S(1)}, bf16[128,4096]{1,0:T(8,128)(2,1)}, u32[]{:S(2)}) copy-start(bf16[128,4096]{1,0:T(8,128)(2,1)} %param.26) | copy-start | bytes 3145732
  63.2 39.2 %all-to-all-start.1 = ((bf16[128,16,256]{2,0,1:T(8,128)(2,1)}), bf16[128,16,256]{2,0,1:T(8,128)(2,1)S(1)}, u32[]{:S(2)}, u32[]{:S(2)}) async-start(bf16[128,16,256]{2,0,1:T(8,128)(2,1)} %bitcast.4), calls=%async_computation.1 | async-start | bytes 2097152 | tf_op jit(solution)/shard_map/all_to_all | solution.py:75
  102.4 37.8 %all-to-all-start.2 = ((bf16[128,16,256]{0,2,1:T(8,128)(2,1)}), bf16[128,16,256]{0,2,1:T(8,128)(2,1)S(1)}, u32[]{:S(2)}, u32[]{:S(2)}) async-start(bf16[128,16,256]{0,2,1:T(8,128)(2,1)} %bitcast.254), calls=%async_computation.2 | async-start | bytes 2097152 | tf_op jit(solution)/shard_map/all_to_all | solution.py:73
  140.3 40.2 %all-to-all-start.3 = ((bf16[128,16,256]{0,2,1:T(8,128)(2,1)}), bf16[128,16,256]{0,2,1:T(8,128)(2,1)}, u32[]{:S(2)}, u32[]{:S(2)}) async-start(bf16[128,16,256]{0,2,1:T(8,128)(2,1)} %bitcast.253), calls=%async_computation.3 | async-start | bytes 2097152 | tf_op jit(solution)/shard_map/all_to_all | solution.py:76
  152.1 48.7 %collective-permute-start = (bf16[2,512,1,256]{3,1,2,0:T(8,128)(2,1)}, bf16[2,512,1,256]{3,1,2,0:T(8,128)(2,1)}, u32[]{:S(2)}, u32[]{:S(2)}) collective-permute-start(bf16[2,512,1,256]{3,1,2,0:T(8,128)(2,1)} %pad_maximum_fusion.4), channel_id=1, source_target_pairs={{0,16},{16,32},{32,48},{48,64},{64,80},{80,96},{96,112},{112,128},... | collective-permute-start | bytes 1572872 | tf_op jit(solution)/shard_map/ppermute | solution.py:19
  159.0 27.8 %copy-start.12 = (bf16[4,128,1,256]{3,1,0,2:T(8,128)(2,1)}, bf16[4,128,1,256]{3,1,0,2:T(8,128)(2,1)S(1)}, u32[]{:S(2)}) copy-start(bf16[4,128,1,256]{3,1,0,2:T(8,128)(2,1)S(1)} %copy.121) | copy-start | bytes 786436
  186.8 2.8 copy-start.22
  186.8 2.8 copy-start.25
  189.6 2.3 copy-start.30
  189.6 2.3 copy-start.14
  189.6 2.3 copy-start.18
  191.9 7.4 %copy-start.3 = (bf16[512,1024]{0,1:T(8,128)(2,1)}, bf16[512,1024]{0,1:T(8,128)(2,1)S(1)}, u32[]{:S(2)}) copy-start(bf16[512,1024]{0,1:T(8,128)(2,1)S(1)} %multiply_convert_fusion.1) | copy-start | bytes 3145732
  193.3 2.3 copy-start.34
  193.4 2.2 copy-start.17
  195.6 4.2 %copy-start.5 = (bf16[512,1024]{0,1:T(8,128)(2,1)}, bf16[512,1024]{0,1:T(8,128)(2,1)S(1)}, u32[]{:S(2)}) copy-start(bf16[512,1024]{0,1:T(8,128)(2,1)S(1)} %multiply_convert_fusion.2) | copy-start | bytes 3145732
  197.0 2.3 copy-start.32
  213.9 41.6 %all-to-all-start.5 = ((bf16[16,2,16384]{2,1,0:T(2,128)(2,1)}), bf16[16,2,16384]{2,1,0:T(2,128)(2,1)S(1)}, u32[]{:S(2)}, u32[]{:S(2)}) async-start(bf16[16,2,16384]{2,1,0:T(2,128)(2,1)} %reshape.765), calls=%async_computation.5 | async-start | bytes 2097152 | tf_op jit(solution)/shard_map/all_to_all | solution.py:121
  236.9 14.2 %collective-permute-start.1 = (f32[2,512,1,256]{3,1,2,0:T(8,128)S(1)}, f32[2,512,1,256]{3,1,2,0:T(8,128)S(1)}, u32[]{:S(2)}, u32[]{:S(2)}) collective-permute-start(f32[2,512,1,256]{3,1,2,0:T(8,128)S(1)} %pad_maximum_fusion.1), channel_id=1, source_target_pairs={{16,0},{32,16},{48,32},{64,48},{80,64},{96,80},{112,96},{128,112},... | collective-permute-start | bytes 3145736 | tf_op jit(solution)/shard_map/ppermute | solution.py:19
  255.5 39.8 %all-to-all-start.6 = ((bf16[16,2,16384]{2,1,0:T(2,128)(2,1)}), bf16[16,2,16384]{2,1,0:T(2,128)(2,1)S(1)}, u32[]{:S(2)}, u32[]{:S(2)}) async-start(bf16[16,2,16384]{2,1,0:T(2,128)(2,1)} %reshape.767), calls=%async_computation.6 | async-start | bytes 2097152 | tf_op jit(solution)/shard_map/all_to_all | solution.py:122
  296.2 40.9 %all-to-all-start.7 = ((bf16[16,2,16384]{2,1,0:T(2,128)(2,1)}), bf16[16,2,16384]{2,1,0:T(2,128)(2,1)}, u32[]{:S(2)}, u32[]{:S(2)}) async-start(bf16[16,2,16384]{2,1,0:T(2,128)(2,1)} %reshape.769), calls=%async_computation.7 | async-start | bytes 2097152 | tf_op jit(solution)/shard_map/all_to_all | solution.py:125
  310.9 3.0 copy-start.1
  (22 other events, 31.6 us)
where the time goes:
time: 345 us; the launch traced here: 343 us
  waiting for transfers between devices  156 us (45%)
  starting transfers between devices  98.1 us (28%)
  local copies, waits for them, and re-layouts  52.1 us (15%)
  matrix products  27.4 us (8%)
  other arithmetic  8.27 us (2%)
    all_to_all x1, waiting for transfers between devices, per_device(): lax.all_to_all(key_heads, 'uly', split_axis=1, concat_axis=0, tiled=True)  27.5 us
    unnamed x87, local copies, waits for them, and re-layouts  27.3 us
    all_to_all x1, waiting for transfers between devices, per_device(): lax.all_to_all(value_heads, 'uly', split_axis=1, concat_axis=0, tiled=True)  26.5 us
    all_to_all x1, waiting for transfers between devices, per_device(): lax.all_to_all(own_key.astype(jnp.bfloat16), 'uly', split_axis=0, concat_...  23.5 us
    all_to_all x1, waiting for transfers between devices, per_device(): lax.all_to_all(query_heads, 'uly', split_axis=1, concat_axis=0, tiled=True)  22.6 us
    all_to_all x1, waiting for transfers between devices, per_device(): lax.all_to_all(own_value.astype(jnp.bfloat16), 'uly', split_axis=0, conca...  20.5 us
    all_to_all x1, waiting for transfers between devices, per_device(): lax.all_to_all(grad_heads, 'uly', split_axis=1, concat_axis=0, tiled=True)  17.1 us
    all_to_all x1, starting transfers between devices, per_device(): lax.all_to_all(row_dot, 'uly', split_axis=1, concat_axis=0, tiled=True)  15.7 us
  transfers between devices with their start and end apart: 10, of which 8 were waited for; matrix products, arithmetic and copies ran while one was open for 17% of the time, Pallas kernels for 0%

commit v1 on v0

v1 whole, which is shorter than its diff:
```python
import functools

import jax
import jax.numpy as jnp
from jax import lax
from jax.experimental import pallas as pl
from jax.experimental.pallas import tpu as pltpu
from jax.sharding import PartitionSpec as P

HEAD_DIM = 256
WINDOW = 512
SCORE_SCALE = 0.0625
SOFT_CAP = 50.0
RING = 8
ROWS = 128
BACK = WINDOW // ROWS
SPAN = (BACK + 1) * ROWS
PAIR = 2 * HEAD_DIM
MESH = pl.DeviceIdType.MESH


def rows_of(index, count=1):
    return pl.ds(pl.multiple_of(index * ROWS, ROWS), count * ROWS)


def cols_of(index, width):
    return pl.ds(pl.multiple_of(index * width, width), width)


def kernel(
    halves,
    query_ref, key_ref, value_ref, grad_ref, dots_ref, seg_ref,
    gq_ref, gk_ref, gv_ref,
    q_buf, d_buf, k_buf, v_buf, kt_buf, r_src, r_buf, seg_buf, low_buf,
    k_acc, v_acc, gq_buf, gkv_buf, halo_out, halo_in,
    send_kv, send_qd, send_r, recv_kv, recv_qd, recv_r, seg_sem,
    halo_send, halo_recv, back_send, back_recv,
    out_send, out_recv,
):
    blk, uly = lax.axis_index("blk"), lax.axis_index("uly")
    side, z = uly // RING, lax.rem(uly, RING)
    half = blk * 2 + side
    has_prev, has_next = half > 0, half < halves - 1

    def device(h, zz):
        return (h // 2, lax.rem(h, 2) * RING + zz)

    def peer_of(offset):
        return lax.rem(z + offset, RING)

    prev_dev, next_dev = device(half - 1, z), device(half + 1, z)

    def key_copy(i):
        src, buf = ((key_ref, k_buf), (value_ref, v_buf))[i]
        return pltpu.make_async_copy(
            src.at[:, cols_of(z, HEAD_DIM)], buf.at[rows_of(BACK + z)], recv_kv.at[i, z]
        )

    def query_copy(i):
        src, buf = ((query_ref, q_buf), (grad_ref, d_buf))[i]
        return pltpu.make_async_copy(
            src.at[:, cols_of(z, PAIR)], buf.at[rows_of(z)], recv_qd.at[i, z]
        )

    for i in range(2):
        key_copy(i).start()
        query_copy(i).start()
    own_seg = pltpu.make_async_copy(seg_ref.at[half], seg_buf.at[1], seg_sem.at[1])
    own_seg.start()

    @pl.when(has_prev)
    def _():
        pltpu.make_async_copy(seg_ref.at[half - 1], seg_buf.at[0], seg_sem.at[0]).start()

    barrier = pltpu.get_barrier_semaphore()
    for offset in range(1, RING):
        pl.semaphore_signal(
            barrier, inc=1, device_id=device(half, peer_of(offset)), device_id_type=MESH
        )

    @pl.when(has_prev)
    def _():
        pl.semaphore_signal(barrier, inc=1, device_id=prev_dev, device_id_type=MESH)

    @pl.when(has_next)
    def _():
        pl.semaphore_signal(barrier, inc=1, device_id=next_dev, device_id_type=MESH)

    dots = dots_ref[...].astype(jnp.float32)
    turned = jnp.concatenate([dots, jnp.zeros((ROWS, ROWS - dots.shape[1]), jnp.float32)], axis=1).T
    for p in range(RING):
        r_src[p] = jnp.concatenate(
            [turned[2 * p : 2 * p + 2], jnp.zeros((6, ROWS), jnp.float32)], axis=0
        )
    r_buf[z] = r_src[z]

    pl.semaphore_wait(
        barrier, RING - 1 + has_prev.astype(jnp.int32) + has_next.astype(jnp.int32)
    )

    def send(src, dst, send_sem, recv_sem, dev):
        return pltpu.make_async_remote_copy(
            src_ref=src, dst_ref=dst, send_sem=send_sem, recv_sem=recv_sem,
            device_id=dev, device_id_type=MESH,
        )

    def send_keys(i, offset):
        src, buf = ((key_ref, k_buf), (value_ref, v_buf))[i]
        p = peer_of(offset)
        return send(
            src.at[:, cols_of(p, HEAD_DIM)], buf.at[rows_of(BACK + z)],
            send_kv.at[i, offset], recv_kv.at[i, z], device(half, p),
        )

    def send_queries(i, offset):
        src, buf = ((query_ref, q_buf), (grad_ref, d_buf))[i]
        p = peer_of(offset)
        return send(
            src.at[:, cols_of(p, PAIR)], buf.at[rows_of(z)],
            send_qd.at[i, offset], recv_qd.at[i, z], device(half, p),
        )

    def send_dots(offset):
        p = peer_of(offset)
        return send(
            r_src.at[p], r_buf.at[z], send_r.at[offset], recv_r.at[z], device(half, p)
        )

    order = (4, 3, 5, 2, 6, 1, 7)
    for offset in order:
        for i in range(2):
            send_keys(i, offset).start()
    for offset in order:
        send_dots(offset).start()
        for i in range(2):
            send_queries(i, offset).start()

    own_seg.wait()

    @pl.when(has_prev)
    def _():
        pltpu.make_async_copy(seg_ref.at[half], seg_buf.at[0], seg_sem.at[0]).wait()

    @pl.when(jnp.logical_not(has_prev))
    def _():
        seg_buf[0] = jnp.full((RING, ROWS), -1, jnp.int32)
        k_buf[: BACK * ROWS] = jnp.zeros((BACK * ROWS, HEAD_DIM), jnp.bfloat16)
        v_buf[: BACK * ROWS] = jnp.zeros((BACK * ROWS, HEAD_DIM), jnp.bfloat16)

    before, here = seg_buf[0], seg_buf[1]
    first = jnp.zeros((RING, ROWS), jnp.int32)
    for doc in range(16):
        below = jnp.sum(
            (before < doc).astype(jnp.int32) + (here < doc).astype(jnp.int32),
            keepdims=True,
        )
        first = jnp.where(here == doc, below, first)
    tile_of = lax.broadcasted_iota(jnp.int32, (RING, ROWS), 0)
    lane_of = lax.broadcasted_iota(jnp.int32, (RING, ROWS), 1)
    origin = (RING - BACK) * ROWS + tile_of * ROWS
    low = jnp.maximum(first - origin, lane_of + 1)
    for t in range(RING):
        low_buf[t] = jnp.broadcast_to(low[t : t + 1], (8, ROWS))

    k_acc[...] = jnp.zeros(k_acc.shape, jnp.float32)
    v_acc[...] = jnp.zeros(v_acc.shape, jnp.float32)

    def wait_keys(j):
        key_slot, value_slot = k_buf.at[rows_of(BACK + j)], v_buf.at[rows_of(BACK + j)]
        pltpu.make_async_copy(key_slot, key_slot, recv_kv.at[0, j]).wait()
        pltpu.make_async_copy(value_slot, value_slot, recv_kv.at[1, j]).wait()

    def turn_keys(index):
        kt_buf[:, rows_of(index)] = k_buf[rows_of(index)].T

    def send_halo(i, j):
        buf = (k_buf, v_buf)[i]
        return send(
            buf.at[rows_of(RING + j)], buf.at[rows_of(j)],
            halo_send.at[i, j], halo_recv.at[i, j], next_dev,
        )

    for j in range(BACK):
        wait_keys(RING - BACK + j)

        @pl.when(has_next)
        def _(j=j):
            send_halo(0, j).start()
            send_halo(1, j).start()

    def turn_late(j, carry):
        turn_keys(RING + j)
        return carry

    lax.fori_loop(0, BACK, turn_late, 0)

    def take_early(j, carry):
        wait_keys(j)
        turn_keys(BACK + j)
        return carry

    lax.fori_loop(0, RING - BACK, take_early, 0)

    @pl.when(has_prev)
    def _():
        for j in range(BACK):
            for i in range(2):
                slot = (k_buf, v_buf)[i].at[rows_of(j)]
                pltpu.make_async_copy(slot, slot, halo_recv.at[i, j]).wait()

    def turn_halo(j, carry):
        turn_keys(j)
        return carry

    lax.fori_loop(0, BACK, turn_halo, 0)

    def send_out(kind, j):
        buf, out, width = (
            (gq_buf.at[rows_of(j)], gq_ref, PAIR),
            (gkv_buf.at[0, rows_of(j)], gk_ref, HEAD_DIM),
            (gkv_buf.at[1, rows_of(j)], gv_ref, HEAD_DIM),
        )[kind]
        dst = out.at[:, cols_of(z, width)]
        remote = send(buf, dst, out_send.at[kind, j], out_recv.at[kind, z], device(half, j))
        local = pltpu.make_async_copy(buf, dst, out_recv.at[kind, z])
        return remote, local

    def start_out(kind, j):
        remote, local = send_out(kind, j)

        @pl.when(j != z)
        def _():
            remote.start()

        @pl.when(j == z)
        def _():
            local.start()

    def nt_dot(a, b):
        return lax.dot_general(
            a, b, (((1,), (1,)), ((), ())), preferred_element_type=jnp.float32
        )

    def dot(a, b):
        return jnp.dot(a, b, preferred_element_type=jnp.float32)

    def finish_keys(j, extra_key, extra_value):
        rows = rows_of(BACK + j)
        gkv_buf[0, rows_of(j)] = (
            (k_acc[rows] * SCORE_SCALE + extra_key).astype(jnp.bfloat16)
        )
        gkv_buf[1, rows_of(j)] = (v_acc[rows] + extra_value).astype(jnp.bfloat16)
        start_out(1, j)
        start_out(2, j)

    def tile(t, carry):
        for i in range(2):
            slot = (q_buf, d_buf)[i].at[rows_of(t)]
            pltpu.make_async_copy(slot, slot, recv_qd.at[i, t]).wait()

        @pl.when(t != z)
        def _():
            pltpu.make_async_copy(r_buf.at[t], r_buf.at[t], recv_r.at[t]).wait()

        span = rows_of(t, BACK + 1)
        queries, grads = q_buf[rows_of(t)], d_buf[rows_of(t)]
        queries = jnp.concatenate([queries[:, :HEAD_DIM], queries[:, HEAD_DIM:]], axis=0)
        grads = jnp.concatenate([grads[:, :HEAD_DIM], grads[:, HEAD_DIM:]], axis=0)
        sums = r_buf[t]
        sums = jnp.concatenate([sums[0:1], sums[1:2]], axis=1)
        least = low_buf[t][0:1]
        least = jnp.concatenate([least, least], axis=1)
        keys = k_buf[span]
        bent = jnp.tanh(nt_dot(keys, queries) * (SCORE_SCALE / SOFT_CAP))
        place = lax.broadcasted_iota(jnp.int32, (SPAN, 2 * ROWS), 0)
        column = lax.broadcasted_iota(jnp.int32, (SPAN, 2 * ROWS), 1)
        most = WINDOW + jnp.where(column < ROWS, column, column - ROWS)
        allowed = (place >= least) & (place <= most)
        weight = jnp.where(allowed, jnp.exp(SOFT_CAP * bent), 0.0)
        prob = weight * (1.0 / jnp.sum(weight, axis=0, keepdims=True))
        grad_prob = nt_dot(v_buf[span], grads)
        grad_score = (prob * (grad_prob - sums) * (1.0 - bent * bent)).astype(jnp.bfloat16)
        v_acc[span] += dot(prob.astype(jnp.bfloat16), grads)
        k_acc[span] += dot(grad_score, queries)
        turned_grad = dot(kt_buf[:, span], grad_score)
        query_grad = (turned_grad * SCORE_SCALE).T.astype(jnp.bfloat16)
        gq_buf[rows_of(t), :HEAD_DIM] = query_grad[:ROWS]
        gq_buf[rows_of(t), HEAD_DIM:] = query_grad[ROWS:]
        start_out(0, t)
        return carry

    def send_back(i):
        return send(
            halo_out.at[i], halo_in.at[i], back_send.at[i], back_recv.at[i], prev_dev
        )

    lax.fori_loop(0, BACK, tile, 0)

    @pl.when(has_prev)
    def _():
        halo_out[0] = (k_acc[: BACK * ROWS] * SCORE_SCALE).astype(jnp.bfloat16)
        halo_out[1] = v_acc[: BACK * ROWS].astype(jnp.bfloat16)
        send_back(0).start()
        send_back(1).start()

    def late_tile(t, carry):
        tile(t, carry)
        finish_keys(t - BACK, 0.0, 0.0)
        return carry

    lax.fori_loop(BACK, RING, late_tile, 0)

    @pl.when(has_next)
    def _():
        for i in range(2):
            pltpu.make_async_copy(halo_in.at[i], halo_in.at[i], back_recv.at[i]).wait()

    @pl.when(jnp.logical_not(has_next))
    def _():
        halo_in[...] = jnp.zeros(halo_in.shape, jnp.bfloat16)

    def last_keys(j, carry):
        rows = rows_of(j)
        finish_keys(
            RING - BACK + j,
            halo_in[0, rows].astype(jnp.float32),
            halo_in[1, rows].astype(jnp.float32),
        )
        return carry

    lax.fori_loop(0, BACK, last_keys, 0)

    for offset in order:
        for i in range(2):
            send_keys(i, offset).wait_send()
            send_queries(i, offset).wait_send()
        send_dots(offset).wait_send()

    @pl.when(has_next)
    def _():
        for j in range(BACK):
            for i in range(2):
                send_halo(i, j).wait_send()

    @pl.when(has_prev)
    def _():
        for i in range(2):
            send_back(i).wait_send()

    def drain(j, carry):
        for kind in range(3):
            remote, _ = send_out(kind, j)

            @pl.when(j != z)
            def _(remote=remote):
                remote.wait_send()

            out, width = ((gq_ref, PAIR), (gk_ref, HEAD_DIM), (gv_ref, HEAD_DIM))[kind]
            landed = out.at[:, cols_of(j, width)]
            pltpu.make_async_copy(landed, landed, out_recv.at[kind, j]).wait()
        return carry

    lax.fori_loop(0, RING, drain, 0)


def per_device(halves, query_in, key_in, value_in, grad_out, row_dot, segments):
    here = pl.BlockSpec(memory_space=pl.ANY)
    low, wide = jnp.bfloat16, jnp.float32
    outs = tuple(jax.ShapeDtypeStruct(a.shape, low) for a in (query_in, key_in, value_in))
    blocks = segments.reshape(halves, RING, ROWS)
    sem = pltpu.SemaphoreType.DMA
    tokens, reach = RING * ROWS, (RING + BACK) * ROWS
    flops = 5 * 2 * RING * SPAN * 2 * ROWS * HEAD_DIM
    return pl.pallas_call(
        functools.partial(kernel, halves),
        out_shape=outs,
        in_specs=[here] * 4 + [pl.BlockSpec(memory_space=pltpu.VMEM), here],
        out_specs=(here,) * 3,
        scratch_shapes=[
            pltpu.VMEM((tokens, PAIR), low),
            pltpu.VMEM((tokens, PAIR), low),
            pltpu.VMEM((reach, HEAD_DIM), low),
            pltpu.VMEM((reach, HEAD_DIM), low),
            pltpu.VMEM((HEAD_DIM, reach), low),
            pltpu.VMEM((RING, 8, ROWS), wide),
            pltpu.VMEM((RING, 8, ROWS), wide),
            pltpu.VMEM((2, RING, ROWS), jnp.int32),
            pltpu.VMEM((RING, 8, ROWS), jnp.int32),
            pltpu.VMEM((reach, HEAD_DIM), wide),
            pltpu.VMEM((reach, HEAD_DIM), wide),
            pltpu.VMEM((tokens, PAIR), low),
            pltpu.VMEM((2, tokens, HEAD_DIM), low),
            pltpu.VMEM((2, BACK * ROWS, HEAD_DIM), low),
            pltpu.VMEM((2, BACK * ROWS, HEAD_DIM), low),
            sem((2, RING)), sem((2, RING)), sem((RING,)),
            sem((2, RING)), sem((2, RING)), sem((RING,)), sem((2,)),
            sem((2, BACK)), sem((2, BACK)), sem((2,)), sem((2,)),
            sem((3, RING)), sem((3, RING)),
        ],
        compiler_params=pltpu.CompilerParams(
            collective_id=0, has_side_effects=True, vmem_limit_bytes=48 * 1024 * 1024
        ),
        cost_estimate=pl.CostEstimate(
            flops=flops, bytes_accessed=5 << 20, transcendentals=2 * RING * SPAN * 2 * ROWS
        ),
        name="window_backward",
    )(query_in, key_in, value_in, grad_out, row_dot, blocks)


def solution(mesh):
    rows = P(("blk", "uly"), None)
    halves = mesh.shape["blk"] * mesh.shape["uly"] // RING
    return jax.shard_map(
        functools.partial(per_device, halves),
        mesh=mesh,
        in_specs=(rows,) * 5 + (P(),),
        out_specs=(rows,) * 3,
        check_vma=False,
    )
```

time: 345 us -> 147 us (0.43)
  the two profiles are of different devices: /device:TPU:40 before, /device:TPU:15 now
where the time goes in v1:
time: 147 us; the launch traced here: 146 us
  Pallas kernels  137 us (93%)
  local copies, waits for them, and re-layouts  8.84 us (6%)
    pallas_call x1, Pallas kernels, per_device(): pl.pallas_call(functools.partial(kernel, halves), out_shape=outs, in_spec...  137 us
    unnamed x14, local copies, waits for them, and re-layouts  8.84 us

profile of v1, /device:TPU:15, one launch (start us, length us, event | category | flops | bytes accessed | tf_op | source)
XLA Modules:
  0.0 146.2 jit_solution(11593445258743012068)
XLA Ops:
  0.6 0.8 copy.9.dots_ref
  1.4 0.0 copy-start
  1.4 1.2 copy-done
  2.7 0.0 copy-start.1
  2.7 1.2 copy-done.1
  3.9 0.0 copy-start.2
  3.9 1.0 copy-done.2
  4.9 0.0 copy-start.3
  4.9 1.0 copy-done.3
  6.0 0.0 copy-start.4
  6.0 0.9 copy-done.4
  6.9 136.7 %window_backward.1 = (bf16[128,4096]{1,0:T(8,128)(2,1)S(1)}, bf16[128,2048]{1,0:T(8,128)(2,1)S(1)}, bf16[128,2048]{1,0:T(8,128)(2,1)S(1)}) custom-call(bf16[128,4096]{1,0:T(8,128)(2,1)S(1)} %copy-done, bf16[128,2048]{1,0:T(8,128)(2,1)S(1)} %copy-done.2, bf16[128,2048]{1,0:T(8,128)(2,1)S(1)} %copy-done.3, bf16[128,4096]{1,0:T(8,128)(2,1)S(1)} %copy-done.1, ...), custom_call_target="tpu_custom_call" | custom-call | flops 3355443200 | bytes 5242880 | tf_op jit(solution)/shard_map/window_backward/pallas_call | solution.py:374
  143.7 1.0 copy.13
  144.6 0.8 copy.14
  145.4 0.8 copy.15
Async XLA Ops:
  1.4 1.2 copy-start
  2.7 1.2 copy-start.1
  3.9 1.0 copy-start.2
  4.9 1.0 copy-start.3
  6.0 0.9 copy-start.4

commit v2 on v1

--- a/solution.py
+++ b/solution.py
@@ -31,7 +31,7 @@
     halves,
     query_ref, key_ref, value_ref, grad_ref, dots_ref, seg_ref,
     gq_ref, gk_ref, gv_ref,
-    q_buf, d_buf, k_buf, v_buf, kt_buf, r_src, r_buf, seg_buf, low_buf,
+    q_buf, d_buf, k_buf, v_buf, kt_buf, dots_buf, r_src, r_buf, seg_buf, low_buf,
     k_acc, v_acc, gq_buf, gkv_buf, halo_out, halo_in,
     send_kv, send_qd, send_r, recv_kv, recv_qd, recv_r, seg_sem,
     halo_send, halo_recv, back_send, back_recv,
@@ -67,6 +67,8 @@
         query_copy(i).start()
     own_seg = pltpu.make_async_copy(seg_ref.at[half], seg_buf.at[1], seg_sem.at[1])
     own_seg.start()
+    dots_copy = pltpu.make_async_copy(dots_ref, dots_buf, seg_sem.at[2])
+    dots_copy.start()
 
     @pl.when(has_prev)
     def _():
@@ -86,8 +88,8 @@
     def _():
         pl.semaphore_signal(barrier, inc=1, device_id=next_dev, device_id_type=MESH)
 
-    dots = dots_ref[...].astype(jnp.float32)
-    turned = jnp.concatenate([dots, jnp.zeros((ROWS, ROWS - dots.shape[1]), jnp.float32)], axis=1).T
+    dots_copy.wait()
+    turned = dots_buf[...].astype(jnp.float32)
     for p in range(RING):
         r_src[p] = jnp.concatenate(
             [turned[2 * p : 2 * p + 2], jnp.zeros((6, ROWS), jnp.float32)], axis=0
@@ -289,19 +291,26 @@
         start_out(0, t)
         return carry
 
-    def send_back(i):
+    def send_back(i, j):
         return send(
-            halo_out.at[i], halo_in.at[i], back_send.at[i], back_recv.at[i], prev_dev
-        )
-
-    lax.fori_loop(0, BACK, tile, 0)
-
-    @pl.when(has_prev)
-    def _():
-        halo_out[0] = (k_acc[: BACK * ROWS] * SCORE_SCALE).astype(jnp.bfloat16)
-        halo_out[1] = v_acc[: BACK * ROWS].astype(jnp.bfloat16)
-        send_back(0).start()
-        send_back(1).start()
+            halo_out.at[i, rows_of(j)], halo_in.at[i, rows_of(j)],
+            back_send.at[i, j], back_recv.at[i, j], prev_dev,
+        )
+
+    def early_tile(t, carry):
+        tile(t, carry)
+
+        @pl.when(has_prev)
+        def _():
+            rows = rows_of(t)
+            halo_out[0, rows] = (k_acc[rows] * SCORE_SCALE).astype(jnp.bfloat16)
+            halo_out[1, rows] = v_acc[rows].astype(jnp.bfloat16)
+            send_back(0, t).start()
+            send_back(1, t).start()
+
+        return carry
+
+    lax.fori_loop(0, BACK, early_tile, 0)
 
     def late_tile(t, carry):
         tile(t, carry)
@@ -310,17 +319,19 @@
 
     lax.fori_loop(BACK, RING, late_tile, 0)
 
-    @pl.when(has_next)
-    def _():
-        for i in range(2):
-            pltpu.make_async_copy(halo_in.at[i], halo_in.at[i], back_recv.at[i]).wait()
-
     @pl.when(jnp.logical_not(has_next))
     def _():
         halo_in[...] = jnp.zeros(halo_in.shape, jnp.bfloat16)
 
     def last_keys(j, carry):
         rows = rows_of(j)
+
+        @pl.when(has_next)
+        def _():
+            for i in range(2):
+                slot = halo_in.at[i, rows]
+                pltpu.make_async_copy(slot, slot, back_recv.at[i, j]).wait()
+
         finish_keys(
             RING - BACK + j,
             halo_in[0, rows].astype(jnp.float32),
@@ -344,8 +355,9 @@
 
     @pl.when(has_prev)
     def _():
-        for i in range(2):
-            send_back(i).wait_send()
+        for j in range(BACK):
+            for i in range(2):
+                send_back(i, j).wait_send()
 
     def drain(j, carry):
         for kind in range(3):
@@ -361,6 +373,24 @@
         return carry
 
     lax.fori_loop(0, RING, drain, 0)
+
+
+def place(*refs):
+    ins, outs, bufs, get, put = refs[:3], refs[3:6], refs[6:9], refs[9], refs[10]
+    parts = [(i, j) for j in range(4) for i in range(3)]
+
+    def step(i, j, out):
+        rows = pl.ds(j * (ROWS // 4), ROWS // 4)
+        src, dst, sems = (bufs[i], outs[i], put) if out else (ins[i], bufs[i], get)
+        return pltpu.make_async_copy(src.at[rows], dst.at[rows], sems.at[i, j])
+
+    for i, j in parts:
+        step(i, j, False).start()
+    for i, j in parts:
+        step(i, j, False).wait()
+        step(i, j, True).start()
+    for i, j in parts:
+        step(i, j, True).wait()
 
 
 def per_device(halves, query_in, key_in, value_in, grad_out, row_dot, segments):
@@ -371,10 +401,10 @@
     sem = pltpu.SemaphoreType.DMA
     tokens, reach = RING * ROWS, (RING + BACK) * ROWS
     flops = 5 * 2 * RING * SPAN * 2 * ROWS * HEAD_DIM
-    return pl.pallas_call(
+    grads = pl.pallas_call(
         functools.partial(kernel, halves),
         out_shape=outs,
-        in_specs=[here] * 4 + [pl.BlockSpec(memory_space=pltpu.VMEM), here],
+        in_specs=[here] * 6,
         out_specs=(here,) * 3,
         scratch_shapes=[
             pltpu.VMEM((tokens, PAIR), low),
@@ -382,6 +412,7 @@
             pltpu.VMEM((reach, HEAD_DIM), low),
             pltpu.VMEM((reach, HEAD_DIM), low),
             pltpu.VMEM((HEAD_DIM, reach), low),
+            pltpu.VMEM((2 * RING, ROWS), low),
             pltpu.VMEM((RING, 8, ROWS), wide),
             pltpu.VMEM((RING, 8, ROWS), wide),
             pltpu.VMEM((2, RING, ROWS), jnp.int32),
@@ -393,18 +424,26 @@
             pltpu.VMEM((2, BACK * ROWS, HEAD_DIM), low),
             pltpu.VMEM((2, BACK * ROWS, HEAD_DIM), low),
             sem((2, RING)), sem((2, RING)), sem((RING,)),
-            sem((2, RING)), sem((2, RING)), sem((RING,)), sem((2,)),
-            sem((2, BACK)), sem((2, BACK)), sem((2,)), sem((2,)),
+            sem((2, RING)), sem((2, RING)), sem((RING,)), sem((3,)),
+            sem((2, BACK)), sem((2, BACK)), sem((2, BACK)), sem((2, BACK)),
             sem((3, RING)), sem((3, RING)),
         ],
         compiler_params=pltpu.CompilerParams(
-            collective_id=0, has_side_effects=True, vmem_limit_bytes=48 * 1024 * 1024
+            collective_id=0, has_side_effects=True, vmem_limit_bytes=62 * 1024 * 1024
         ),
         cost_estimate=pl.CostEstimate(
             flops=flops, bytes_accessed=5 << 20, transcendentals=2 * RING * SPAN * 2 * ROWS
         ),
         name="window_backward",
-    )(query_in, key_in, value_in, grad_out, row_dot, blocks)
+    )(query_in, key_in, value_in, grad_out, row_dot.T, blocks)
+    return pl.pallas_call(
+        place,
+        out_shape=outs,
+        in_specs=[here] * 3,
+        out_specs=(here,) * 3,
+        scratch_shapes=[pltpu.VMEM(o.shape, low) for o in outs] + [sem((3, 4))] * 2,
+        name="place",
+    )(*grads)
 
 
 def solution(mesh):

time: 147 us -> 135 us (0.918)
  the two profiles are of different devices: /device:TPU:15 before, /device:TPU:53 now
where the time goes in v2:
time: 135 us
  Pallas kernels  135 us (100%)
    pallas_call x1, Pallas kernels, per_device(): pl.pallas_call(functools.partial(kernel, halves), out_shape=outs, in_spec...  132 us

profile of v2, /device:TPU:53, one launch (start us, length us, event | category | flops | bytes accessed | tf_op | source)
XLA Modules:
  0.0 135.3 jit_solution(8367677612796963197)
XLA Ops:
  0.6 132.2 %window_backward.1 = (bf16[128,4096]{1,0:T(8,128)(2,1)}, bf16[128,2048]{1,0:T(8,128)(2,1)}, bf16[128,2048]{1,0:T(8,128)(2,1)}) custom-call(bf16[128,4096]{1,0:T(8,128)(2,1)} %query_ref.1, bf16[128,2048]{1,0:T(8,128)(2,1)} %key_ref.1, bf16[128,2048]{1,0:T(8,128)(2,1)} %value_ref.1, bf16[128,4096]{1,0:T(8,128)(2,1)} %grad_ref.1, bf16[16,128]{1,0:T(8,128)(2,1)} %bitcast.3, ...), custom_call_target="tpu_custom_call" | custom-call | flops 3355443200 | bytes 5242880 | tf_op jit(solution)/shard_map/window_backward/pallas_call | solution.py:404
  132.8 2.5 %place.1 = (bf16[128,4096]{1,0:T(8,128)(2,1)}, bf16[128,2048]{1,0:T(8,128)(2,1)}, bf16[128,2048]{1,0:T(8,128)(2,1)}) custom-call(bf16[128,4096]{1,0:T(8,128)(2,1)} %get-tuple-element.6.refs_0_, bf16[128,2048]{1,0:T(8,128)(2,1)} %get-tuple-element.7.refs_1_, bf16[128,2048]{1,0:T(8,128)(2,1)} %get-tuple-element.8.refs_2_), custom_call_target="tpu_custom_call" | custom-call | tf_op jit(solution)/shard_map/place/pallas_call | solution.py:439

commit v3 on v2

--- a/solution.py
+++ b/solution.py
@@ -50,6 +50,20 @@
 
     prev_dev, next_dev = device(half - 1, z), device(half + 1, z)
 
+    barrier = pltpu.get_barrier_semaphore()
+    for offset in range(1, RING):
+        pl.semaphore_signal(
+            barrier, inc=1, device_id=device(half, peer_of(offset)), device_id_type=MESH
+        )
+
+    @pl.when(has_prev)
+    def _():
+        pl.semaphore_signal(barrier, inc=1, device_id=prev_dev, device_id_type=MESH)
+
+    @pl.when(has_next)
+    def _():
+        pl.semaphore_signal(barrier, inc=1, device_id=next_dev, device_id_type=MESH)
+
     def key_copy(i):
         src, buf = ((key_ref, k_buf), (value_ref, v_buf))[i]
         return pltpu.make_async_copy(
@@ -74,20 +88,6 @@
     def _():
         pltpu.make_async_copy(seg_ref.at[half - 1], seg_buf.at[0], seg_sem.at[0]).start()
 
-    barrier = pltpu.get_barrier_semaphore()
-    for offset in range(1, RING):
-        pl.semaphore_signal(
-            barrier, inc=1, device_id=device(half, peer_of(offset)), device_id_type=MESH
-        )
-
-    @pl.when(has_prev)
-    def _():
-        pl.semaphore_signal(barrier, inc=1, device_id=prev_dev, device_id_type=MESH)
-
-    @pl.when(has_next)
-    def _():
-        pl.semaphore_signal(barrier, inc=1, device_id=next_dev, device_id_type=MESH)
-
     dots_copy.wait()
     turned = dots_buf[...].astype(jnp.float32)
     for p in range(RING):
@@ -128,7 +128,7 @@
             r_src.at[p], r_buf.at[z], send_r.at[offset], recv_r.at[z], device(half, p)
         )
 
-    order = (4, 3, 5, 2, 6, 1, 7)
+    order = (1, 7, 2, 6, 3, 5, 4)
     for offset in order:
         for i in range(2):
             send_keys(i, offset).start()
@@ -297,27 +297,42 @@
             back_send.at[i, j], back_recv.at[i, j], prev_dev,
         )
 
-    def early_tile(t, carry):
+    def step_of(t):
+        ahead = lax.rem(t - z + RING, RING)
+        return jnp.where(ahead * 2 <= RING, jnp.maximum(2 * ahead - 1, 0), 2 * (RING - ahead))
+
+    def done_at(first, last):
+        at = step_of(first)
+        for t in range(first + 1, last + 1):
+            at = jnp.maximum(at, step_of(t))
+        return at
+
+    halo_done = [done_at(0, j) for j in range(BACK)]
+    own_done = [done_at(j, j + BACK) for j in range(RING - BACK)]
+
+    def one_step(step, carry):
+        near = (step + 1) // 2
+        t = lax.rem(z + jnp.where(lax.rem(step, 2) == 1, near, RING - near), RING)
         tile(t, carry)
-
-        @pl.when(has_prev)
-        def _():
-            rows = rows_of(t)
-            halo_out[0, rows] = (k_acc[rows] * SCORE_SCALE).astype(jnp.bfloat16)
-            halo_out[1, rows] = v_acc[rows].astype(jnp.bfloat16)
-            send_back(0, t).start()
-            send_back(1, t).start()
-
-        return carry
-
-    lax.fori_loop(0, BACK, early_tile, 0)
-
-    def late_tile(t, carry):
-        tile(t, carry)
-        finish_keys(t - BACK, 0.0, 0.0)
-        return carry
-
-    lax.fori_loop(BACK, RING, late_tile, 0)
+        for j in range(BACK):
+
+            @pl.when((halo_done[j] == step) & has_prev)
+            def _(j=j):
+                rows = rows_of(j)
+                halo_out[0, rows] = (k_acc[rows] * SCORE_SCALE).astype(jnp.bfloat16)
+                halo_out[1, rows] = v_acc[rows].astype(jnp.bfloat16)
+                send_back(0, j).start()
+                send_back(1, j).start()
+
+        for j in range(RING - BACK):
+
+            @pl.when(own_done[j] == step)
+            def _(j=j):
+                finish_keys(j, 0.0, 0.0)
+
+        return carry
+
+    lax.fori_loop(0, RING, one_step, 0)
 
     @pl.when(jnp.logical_not(has_next))
     def _():

time: 135 us -> 133 us (0.985)
  the two profiles are of different devices: /device:TPU:53 before, /device:TPU:68 now
where the time goes in v3:
time: 133 us
  Pallas kernels  132 us (99%)
    pallas_call x1, Pallas kernels, per_device(): pl.pallas_call(functools.partial(kernel, halves), out_shape=outs, in_spec...  130 us

profile of v3, /device:TPU:68, one launch (start us, length us, event | category | flops | bytes accessed | tf_op | source)
XLA Modules:
  0.0 132.8 jit_solution(15130179846824163455)
XLA Ops:
  0.6 129.7 %window_backward.1 = (bf16[128,4096]{1,0:T(8,128)(2,1)}, bf16[128,2048]{1,0:T(8,128)(2,1)}, bf16[128,2048]{1,0:T(8,128)(2,1)}) custom-call(bf16[128,4096]{1,0:T(8,128)(2,1)} %query_ref.1, bf16[128,2048]{1,0:T(8,128)(2,1)} %key_ref.1, bf16[128,2048]{1,0:T(8,128)(2,1)} %value_ref.1, bf16[128,4096]{1,0:T(8,128)(2,1)} %grad_ref.1, bf16[16,128]{1,0:T(8,128)(2,1)} %bitcast.3, ...), custom_call_target="tpu_custom_call" | custom-call | flops 3355443200 | bytes 5242880 | tf_op jit(solution)/shard_map/window_backward/pallas_call | solution.py:419
  130.3 2.5 %place.1 = (bf16[128,4096]{1,0:T(8,128)(2,1)}, bf16[128,2048]{1,0:T(8,128)(2,1)}, bf16[128,2048]{1,0:T(8,128)(2,1)}) custom-call(bf16[128,4096]{1,0:T(8,128)(2,1)} %get-tuple-element.6.refs_0_, bf16[128,2048]{1,0:T(8,128)(2,1)} %get-tuple-element.7.refs_1_, bf16[128,2048]{1,0:T(8,128)(2,1)} %get-tuple-element.8.refs_2_), custom_call_target="tpu_custom_call" | custom-call | tf_op jit(solution)/shard_map/place/pallas_call | solution.py:454

commit v4 on v3

--- a/solution.py
+++ b/solution.py
@@ -9,6 +9,8 @@
 
 HEAD_DIM = 256
 WINDOW = 512
+LEAD = 3
+ORDER = (1, 7, 2, 6, 3, 5, 4)
 SCORE_SCALE = 0.0625
 SOFT_CAP = 50.0
 RING = 8
@@ -35,7 +37,7 @@
     k_acc, v_acc, gq_buf, gkv_buf, halo_out, halo_in,
     send_kv, send_qd, send_r, recv_kv, recv_qd, recv_r, seg_sem,
     halo_send, halo_recv, back_send, back_recv,
-    out_send, out_recv,
+    out_send, out_recv, ring_sem, halo_sem,
 ):
     blk, uly = lax.axis_index("blk"), lax.axis_index("uly")
     side, z = uly // RING, lax.rem(uly, RING)
@@ -51,18 +53,18 @@
     prev_dev, next_dev = device(half - 1, z), device(half + 1, z)
 
     barrier = pltpu.get_barrier_semaphore()
+    lead = z == LEAD
+
+    def ring_signal(sem, offset):
+        pl.semaphore_signal(
+            sem, inc=1, device_id=device(half, peer_of(offset)), device_id_type=MESH
+        )
+
     for offset in range(1, RING):
-        pl.semaphore_signal(
-            barrier, inc=1, device_id=device(half, peer_of(offset)), device_id_type=MESH
-        )
-
-    @pl.when(has_prev)
-    def _():
-        pl.semaphore_signal(barrier, inc=1, device_id=prev_dev, device_id_type=MESH)
-
-    @pl.when(has_next)
-    def _():
-        pl.semaphore_signal(barrier, inc=1, device_id=next_dev, device_id_type=MESH)
+
+        @pl.when(peer_of(offset) != LEAD)
+        def _(offset=offset):
+            ring_signal(barrier, offset)
 
     def key_copy(i):
         src, buf = ((key_ref, k_buf), (value_ref, v_buf))[i]
@@ -96,9 +98,22 @@
         )
     r_buf[z] = r_src[z]
 
-    pl.semaphore_wait(
-        barrier, RING - 1 + has_prev.astype(jnp.int32) + has_next.astype(jnp.int32)
-    )
+    @pl.when(jnp.logical_not(lead))
+    def _():
+        pl.semaphore_wait(barrier, RING - 1)
+        pl.semaphore_signal(ring_sem, inc=1, device_id=device(half, LEAD), device_id_type=MESH)
+
+    @pl.when(lead)
+    def _():
+        pl.semaphore_wait(ring_sem, RING - 1)
+
+        @pl.when(has_prev)
+        def _():
+            pl.semaphore_signal(barrier, inc=1, device_id=prev_dev, device_id_type=MESH)
+
+        @pl.when(has_next)
+        def _():
+            pl.semaphore_signal(barrier, inc=1, device_id=next_dev, device_id_type=MESH)
 
     def send(src, dst, send_sem, recv_sem, dev):
         return pltpu.make_async_remote_copy(
@@ -125,10 +140,10 @@
     def send_dots(offset):
         p = peer_of(offset)
         return send(
-            r_src.at[p], r_buf.at[z], send_r.at[offset], recv_r.at[z], device(half, p)
-        )
-
-    order = (1, 7, 2, 6, 3, 5, 4)
+            r_src.at[p, :2], r_buf.at[z, :2], send_r.at[offset], recv_r.at[z], device(half, p)
+        )
+
+    order = ORDER
     for offset in order:
         for i in range(2):
             send_keys(i, offset).start()
@@ -181,6 +196,16 @@
             buf.at[rows_of(RING + j)], buf.at[rows_of(j)],
             halo_send.at[i, j], halo_recv.at[i, j], next_dev,
         )
+
+    @pl.when(lead)
+    def _():
+        pl.semaphore_wait(barrier, has_prev.astype(jnp.int32) + has_next.astype(jnp.int32))
+        for offset in range(1, RING):
+            ring_signal(halo_sem, offset)
+
+    @pl.when(jnp.logical_not(lead))
+    def _():
+        pl.semaphore_wait(halo_sem, 1)
 
     for j in range(BACK):
         wait_keys(RING - BACK + j)
@@ -262,7 +287,7 @@
 
         @pl.when(t != z)
         def _():
-            pltpu.make_async_copy(r_buf.at[t], r_buf.at[t], recv_r.at[t]).wait()
+            pltpu.make_async_copy(r_buf.at[t, :2], r_buf.at[t, :2], recv_r.at[t]).wait()
 
         span = rows_of(t, BACK + 1)
         queries, grads = q_buf[rows_of(t)], d_buf[rows_of(t)]
@@ -298,8 +323,10 @@
         )
 
     def step_of(t):
-        ahead = lax.rem(t - z + RING, RING)
-        return jnp.where(ahead * 2 <= RING, jnp.maximum(2 * ahead - 1, 0), 2 * (RING - ahead))
+        ahead, at = lax.rem(t - z + RING, RING), 0
+        for step, offset in enumerate(order, 1):
+            at = jnp.where(ahead == RING - offset, step, at)
+        return at
 
     def done_at(first, last):
         at = step_of(first)
@@ -311,8 +338,10 @@
     own_done = [done_at(j, j + BACK) for j in range(RING - BACK)]
 
     def one_step(step, carry):
-        near = (step + 1) // 2
-        t = lax.rem(z + jnp.where(lax.rem(step, 2) == 1, near, RING - near), RING)
+        ahead = 0
+        for at, offset in enumerate(order, 1):
+            ahead = jnp.where(step == at, RING - offset, ahead)
+        t = lax.rem(z + ahead, RING)
         tile(t, carry)
         for j in range(BACK):
 
@@ -324,15 +353,15 @@
                 send_back(0, j).start()
                 send_back(1, j).start()
 
-        for j in range(RING - BACK):
-
-            @pl.when(own_done[j] == step)
-            def _(j=j):
-                finish_keys(j, 0.0, 0.0)
-
         return carry
 
     lax.fori_loop(0, RING, one_step, 0)
+
+    def first_keys(j, carry):
+        finish_keys(j, 0.0, 0.0)
+        return carry
+
+    lax.fori_loop(0, RING - BACK, first_keys, 0)
 
     @pl.when(jnp.logical_not(has_next))
     def _():
@@ -442,6 +471,7 @@
             sem((2, RING)), sem((2, RING)), sem((RING,)), sem((3,)),
             sem((2, BACK)), sem((2, BACK)), sem((2, BACK)), sem((2, BACK)),
             sem((3, RING)), sem((3, RING)),
+            pltpu.SemaphoreType.REGULAR, pltpu.SemaphoreType.REGULAR,
         ],
         compiler_params=pltpu.CompilerParams(
             collective_id=0, has_side_effects=True, vmem_limit_bytes=62 * 1024 * 1024

time: 133 us -> 128 us (0.962)
  the two profiles are of different devices: /device:TPU:68 before, /device:TPU:78 now
where the time goes in v4:
time: 128 us
  Pallas kernels  127 us (99%)
    pallas_call x1, Pallas kernels, per_device(): pl.pallas_call(functools.partial(kernel, halves), out_shape=outs, in_spec...  125 us

profile of v4, /device:TPU:78, one launch (start us, length us, event | category | flops | bytes accessed | tf_op | source)
XLA Modules:
  0.0 127.7 jit_solution(15190965355763427941)
XLA Ops:
  0.6 124.6 %window_backward.1 = (bf16[128,4096]{1,0:T(8,128)(2,1)}, bf16[128,2048]{1,0:T(8,128)(2,1)}, bf16[128,2048]{1,0:T(8,128)(2,1)}) custom-call(bf16[128,4096]{1,0:T(8,128)(2,1)} %query_ref.1, bf16[128,2048]{1,0:T(8,128)(2,1)} %key_ref.1, bf16[128,2048]{1,0:T(8,128)(2,1)} %value_ref.1, bf16[128,4096]{1,0:T(8,128)(2,1)} %grad_ref.1, bf16[16,128]{1,0:T(8,128)(2,1)} %bitcast.3, ...), custom_call_target="tpu_custom_call" | custom-call | flops 3355443200 | bytes 5242880 | tf_op jit(solution)/shard_map/window_backward/pallas_call | solution.py:448
  125.2 2.5 %place.1 = (bf16[128,4096]{1,0:T(8,128)(2,1)}, bf16[128,2048]{1,0:T(8,128)(2,1)}, bf16[128,2048]{1,0:T(8,128)(2,1)}) custom-call(bf16[128,4096]{1,0:T(8,128)(2,1)} %get-tuple-element.6.refs_0_, bf16[128,2048]{1,0:T(8,128)(2,1)} %get-tuple-element.7.refs_1_, bf16[128,2048]{1,0:T(8,128)(2,1)} %get-tuple-element.8.refs_2_), custom_call_target="tpu_custom_call" | custom-call | tf_op jit(solution)/shard_map/place/pallas_call | solution.py:484

commit v5 on v4

--- a/solution.py
+++ b/solution.py
@@ -10,7 +10,7 @@
 HEAD_DIM = 256
 WINDOW = 512
 LEAD = 3
-ORDER = (1, 7, 2, 6, 3, 5, 4)
+ORDER = (1, 7, 4, 3, 5, 2, 6)
 SCORE_SCALE = 0.0625
 SOFT_CAP = 50.0
 RING = 8
@@ -361,7 +361,8 @@
         finish_keys(j, 0.0, 0.0)
         return carry
 
-    lax.fori_loop(0, RING - BACK, first_keys, 0)
+    for j in (1, 0, 2, 3):
+        first_keys(j, 0)
 
     @pl.when(jnp.logical_not(has_next))
     def _():

time: 128 us -> 127 us (level)
  the two profiles are of different devices: /device:TPU:78 before, /device:TPU:190 now
where the time goes in v5:
time: 127 us
  Pallas kernels  126 us (99%)
    pallas_call x1, Pallas kernels, per_device(): pl.pallas_call(functools.partial(kernel, halves), out_shape=outs, in_spec...  124 us

profile of v5, /device:TPU:190, one launch (start us, length us, event | category | flops | bytes accessed | tf_op | source)
XLA Modules:
  0.0 127.0 jit_solution(11380721576466200843)
XLA Ops:
  0.6 123.9 %window_backward.1 = (bf16[128,4096]{1,0:T(8,128)(2,1)}, bf16[128,2048]{1,0:T(8,128)(2,1)}, bf16[128,2048]{1,0:T(8,128)(2,1)}) custom-call(bf16[128,4096]{1,0:T(8,128)(2,1)} %query_ref.1, bf16[128,2048]{1,0:T(8,128)(2,1)} %key_ref.1, bf16[128,2048]{1,0:T(8,128)(2,1)} %value_ref.1, bf16[128,4096]{1,0:T(8,128)(2,1)} %grad_ref.1, bf16[16,128]{1,0:T(8,128)(2,1)} %bitcast.3, ...), custom_call_target="tpu_custom_call" | custom-call | flops 3355443200 | bytes 5242880 | tf_op jit(solution)/shard_map/window_backward/pallas_call | solution.py:449
  124.5 2.5 %place.1 = (bf16[128,4096]{1,0:T(8,128)(2,1)}, bf16[128,2048]{1,0:T(8,128)(2,1)}, bf16[128,2048]{1,0:T(8,128)(2,1)}) custom-call(bf16[128,4096]{1,0:T(8,128)(2,1)} %get-tuple-element.6.refs_0_, bf16[128,2048]{1,0:T(8,128)(2,1)} %get-tuple-element.7.refs_1_, bf16[128,2048]{1,0:T(8,128)(2,1)} %get-tuple-element.8.refs_2_), custom_call_target="tpu_custom_call" | custom-call | tf_op jit(solution)/shard_map/place/pallas_call | solution.py:485

commit v6 on v5

--- a/solution.py
+++ b/solution.py
@@ -90,14 +90,6 @@
     def _():
         pltpu.make_async_copy(seg_ref.at[half - 1], seg_buf.at[0], seg_sem.at[0]).start()
 
-    dots_copy.wait()
-    turned = dots_buf[...].astype(jnp.float32)
-    for p in range(RING):
-        r_src[p] = jnp.concatenate(
-            [turned[2 * p : 2 * p + 2], jnp.zeros((6, ROWS), jnp.float32)], axis=0
-        )
-    r_buf[z] = r_src[z]
-
     @pl.when(jnp.logical_not(lead))
     def _():
         pl.semaphore_wait(barrier, RING - 1)
@@ -147,6 +139,14 @@
     for offset in order:
         for i in range(2):
             send_keys(i, offset).start()
+    dots_copy.wait()
+    turned = dots_buf[...].astype(jnp.float32)
+    for p in range(RING):
+        r_src[p] = jnp.concatenate(
+            [turned[2 * p : 2 * p + 2], jnp.zeros((6, ROWS), jnp.float32)], axis=0
+        )
+    r_buf[z] = r_src[z]
+
     for offset in order:
         send_dots(offset).start()
         for i in range(2):

time: 127 us -> 127 us (level)
  no operation moved by 1% of the time
where the time goes in v6:
time: 127 us; the launch traced here: 126 us
  Pallas kernels  126 us (99%)
    pallas_call x1, Pallas kernels, per_device(): pl.pallas_call(functools.partial(kernel, halves), out_shape=outs, in_spec...  123 us

profile of v6, /device:TPU:190, one launch (start us, length us, event | category | flops | bytes accessed | tf_op | source)
XLA Modules:
  0.0 126.4 jit_solution(9178435788231087716)
XLA Ops:
  0.6 123.3 %window_backward.1 = (bf16[128,4096]{1,0:T(8,128)(2,1)}, bf16[128,2048]{1,0:T(8,128)(2,1)}, bf16[128,2048]{1,0:T(8,128)(2,1)}) custom-call(bf16[128,4096]{1,0:T(8,128)(2,1)} %query_ref.1, bf16[128,2048]{1,0:T(8,128)(2,1)} %key_ref.1, bf16[128,2048]{1,0:T(8,128)(2,1)} %value_ref.1, bf16[128,4096]{1,0:T(8,128)(2,1)} %grad_ref.1, bf16[16,128]{1,0:T(8,128)(2,1)} %bitcast.3, ...), custom_call_target="tpu_custom_call" | custom-call | flops 3355443200 | bytes 5242880 | tf_op jit(solution)/shard_map/window_backward/pallas_call | solution.py:449
  123.9 2.5 %place.1 = (bf16[128,4096]{1,0:T(8,128)(2,1)}, bf16[128,2048]{1,0:T(8,128)(2,1)}, bf16[128,2048]{1,0:T(8,128)(2,1)}) custom-call(bf16[128,4096]{1,0:T(8,128)(2,1)} %get-tuple-element.6.refs_0_, bf16[128,2048]{1,0:T(8,128)(2,1)} %get-tuple-element.7.refs_1_, bf16[128,2048]{1,0:T(8,128)(2,1)} %get-tuple-element.8.refs_2_), custom_call_target="tpu_custom_call" | custom-call | tf_op jit(solution)/shard_map/place/pallas_call | solution.py:485
